TPU v7x, 256 devices: a whole 4x4x8 slice. The times are simulated.
256 devices in a mesh: head: 8 (over x, core), expert: 32 (over z, y).
Axes of the slice: x: 4, y: 4, z: 8, core: 2. Of those that a mesh axis runs over, the one named last changes fastest.
Arguments:
- queries: bfloat16 [512, 128, 576], P('expert', 'head'), may hold values from -64 to 64
- resident_cache: bfloat16 [128, 256, 576], P('expert'), may hold values from -6 to 6
- resident_len: int32 [128], P('expert'), may hold values from 1 to 256, as said below
- new_cache: bfloat16 [384, 64, 576], P('expert'), may hold values from -6 to 6
- new_len: int32 [384], replicated, may hold values from 1 to 64, as said below
- new_owner: int32 [384], replicated, may hold values from 0 to 31, as said below
- value_up: bfloat16 [128, 512, 128], P('head'), may hold values from -0.25 to 0.25
- w_output: bfloat16 [16384, 7168], P('head', 'expert'), may hold values from -0.046875 to 0.046875
- residual: bfloat16 [512, 7168], P(None, 'expert'), may hold values from -6 to 6
- expert_ids: int32 [512, 8], replicated, may hold values from 0 to 31, all different within a row; in each aligned block of 16 rows (0 to 15, 16 to 31, ...) at most 6 rows name the same one
- expert_gates: float32 [512, 8], replicated, may hold values from 0.1 to 1
- norm_gain: bfloat16 [7168], replicated, may hold values from 0.5 to 1.5
- w_gate: bfloat16 [32, 7168, 1024], P('expert', None, 'head'), may hold values from -0.0625 to 0.0625
- w_up: bfloat16 [32, 7168, 1024], P('expert', None, 'head'), may hold values from -0.0625 to 0.0625
- w_down: bfloat16 [32, 1024, 7168], P('expert', 'head'), may hold values from -0.1875 to 0.1875
Outputs:
- layer_out: bfloat16 [512, 7168], P('head', 'expert')
Inputs may be any that keep to these rules, and one draw needn't show every extreme that they name: `resident_len`: every decode owner has a resident request of length 256. `new_len`: every prefill device holds a new request of length 64. `new_owner`: one prefill device sends at most 2 of its 12 new requests to one decode owner, and every decode owner receives exactly 12 in all; a prefill device sends either 2 or none to each owner, except to at most one owner, which gets the remainder of 12 divided by 2. `expert_ids`: in each aligned block of 16 rows (the rows of one decode owner) no expert is named by more than 6 rows; the 8 experts of a row differ.
All inputs are finite; a program needn't handle non-finite values.
Results may differ from a plain program's by a relative error of at most 0.012.
Values may be sent and summed in bfloat16 or wider, within the bound.
No kernel may reach another device: no remote copies, remote signals or barrier semaphores. Data moves between devices by JAX's collectives and lax.ppermute only.
A program may use at most 128 MiB of HBM per device.

v0:
```python
import jax
import jax.numpy as jnp
from jax import lax
from jax.sharding import Mesh
from jax.sharding import PartitionSpec as P

ROPE = 64
NOPE = 128
EXPERT = ("expert_0", "expert_1")
HEAD = ("head_0", "head_1")


def whole_of(x, axes, dim):
    if not axes:
        return x
    nearer = lax.all_gather(x, axes[-1], axis=dim, tiled=True)
    return whole_of(nearer, axes[:-1], dim)


def split_up(x, dim, peers):
    dims = x.shape
    pieces = x.reshape(*dims[:dim], peers, dims[dim] // peers, *dims[dim + 1 :])
    return jnp.moveaxis(pieces, dim, 0)


def sent_and_summed(x, axis, dim):
    pieces = split_up(x, dim, lax.axis_size(axis))
    arrived = lax.all_to_all(pieces, axis, split_axis=0, concat_axis=0, tiled=True)
    return arrived.sum(axis=0)


def cut_rows(length, count):
    hop = length // count
    if hop >= 8:
        hop -= hop % 8
    return [hop * k for k in range(1, count)]


def gather_in_order(x, axes, sequence):
    pieces = x
    for k in sequence:
        pieces = lax.all_gather(pieces, axes[k])
    done = sequence[::-1]
    back = [done.index(k) for k in range(len(axes))]
    pieces = pieces.transpose(*back, *range(len(axes), pieces.ndim))
    return pieces.reshape(-1, *x.shape)


def joined_along(pieces, dim):
    pieces = jnp.moveaxis(pieces, 0, dim)
    dims = pieces.shape
    return pieces.reshape(*dims[:dim], dims[dim] * dims[dim + 1], *dims[dim + 2 :])


def gather_all_axes(x, axes, dim):
    split_at = max(range(max(1, x.ndim - 1)), key=lambda d: x.shape[d])
    count, gathered = (len(axes), [])
    for initial, slab in enumerate(jnp.split(x, cut_rows(x.shape[split_at], count), axis=split_at)):
        if slab.size:
            sequence = [(initial - k) % count for k in range(count)]
            gathered.append(gather_in_order(slab, axes, sequence))
    return joined_along(jnp.concatenate(gathered, axis=split_at + 1), dim)


def attend(queries, caches, length, value_up):
    inverse_root = (NOPE + ROPE) ** (-0.5)
    latent_width = value_up.shape[1]
    scores = (
        jnp.einsum("rhc,rtc->rht", queries, caches, preferred_element_type=jnp.float32)
        * inverse_root
    )
    inside = lax.broadcasted_iota(jnp.int32, scores.shape, 2) < length[:, None, None]
    scores = jnp.where(inside, scores, -jnp.inf)
    highest = jnp.max(scores, axis=2, keepdims=True)
    raised = jnp.exp(scores - highest)
    weights = (raised / jnp.sum(raised, axis=2, keepdims=True)).astype(jnp.bfloat16)
    latent = jnp.einsum(
        "rht,rtc->rhc", weights, caches[:, :, :latent_width], preferred_element_type=jnp.float32
    ).astype(jnp.bfloat16)
    values = jnp.einsum(
        "rhc,hcv->rhv", latent, value_up, preferred_element_type=jnp.float32
    ).astype(jnp.bfloat16)
    return values.reshape(values.shape[0], -1)


def earlier_equal(labels):
    count = labels.shape[0]
    position = jnp.arange(count, dtype=jnp.int32)
    before = (labels[:, None] == labels[None, :]) & (position[None, :] < position[:, None])
    return jnp.sum(before.astype(jnp.int32), axis=1)


def per_device(
    queries,
    resident_cache,
    resident_len,
    new_cache,
    new_len,
    new_owner,
    value_up,
    w_output,
    residual,
    expert_ids,
    expert_gates,
    norm_gain,
    w_gate,
    w_up,
    w_down,
):
    n_expert = lax.axis_size(EXPERT)
    n_head = lax.axis_size(HEAD)
    owner_index = lax.axis_index(EXPERT)
    head_index = lax.axis_index(HEAD)
    req_count = resident_cache.shape[0]
    new_count = new_cache.shape[0]
    rows_dev = req_count + new_count
    rows_all = rows_dev * n_expert
    choose = expert_ids.shape[1]
    local_experts = w_gate.shape[0]
    experts = local_experts * n_expert
    column_slab = residual.shape[1]
    most = max(2, (4 * new_count + 3 * n_expert - 1) // (3 * n_expert))
    capacity = max(2, 3 * rows_dev * choose // (2 * experts))
    slots_all = n_expert * capacity
    group = n_expert // n_head
    block_rows = group * rows_dev
    cache_shape = new_cache.shape[1:]
    targets = lax.dynamic_slice_in_dim(new_owner, owner_index * new_count, new_count)
    places = targets * most + earlier_equal(targets)
    senders = (
        jnp.full((n_expert * most,), new_count, jnp.int32)
        .at[places]
        .set(jnp.arange(new_count, dtype=jnp.int32))
    )
    outgoing = jnp.take(new_cache, senders, axis=0, mode="fill", fill_value=0).reshape(
        (n_expert, most) + cache_shape
    )
    span = cache_shape[0] // n_head
    position_block = lax.dynamic_slice_in_dim(outgoing, head_index * span, span, 2)
    moved = lax.all_to_all(position_block, EXPERT, split_axis=0, concat_axis=0, tiled=True)
    incoming = lax.all_gather(moved, HEAD, axis=2, tiled=True)
    ordering = jnp.argsort(new_owner, stable=True)
    chosen = lax.dynamic_slice_in_dim(ordering, owner_index * new_count, new_count)
    anchor = chosen // new_count
    arrived = jnp.take(
        incoming.reshape((n_expert * most,) + cache_shape),
        anchor * most + earlier_equal(anchor),
        axis=0,
    )
    resident_att = attend(queries[:req_count], resident_cache, resident_len, value_up)
    arrived_att = attend(queries[req_count:], arrived, new_len[chosen], value_up)
    attention = jnp.concatenate([resident_att, arrived_att], axis=0)
    mixed = jnp.dot(whole_of(attention, EXPERT, 0), w_output, preferred_element_type=jnp.float32)
    picks = expert_ids.reshape(n_expert, rows_dev * choose)
    onehot = (picks[:, :, None] == jnp.arange(experts, dtype=jnp.int32)[None, None, :]).astype(
        jnp.int32
    )
    ranking = jnp.sum(jnp.cumsum(onehot, axis=1) * onehot, axis=2) - 1
    source = jnp.broadcast_to(jnp.arange(n_expert, dtype=jnp.int32)[:, None], picks.shape)
    slot_index = picks * slots_all + source * capacity + ranking
    row_index = (
        source * rows_dev + jnp.arange(rows_dev * choose, dtype=jnp.int32)[None, :] // choose
    )
    slot_rows = (
        jnp.full((experts * slots_all,), rows_all, jnp.int32)
        .at[slot_index.reshape(-1)]
        .set(row_index.reshape(-1))
    )
    share = sent_and_summed(mixed, HEAD, 0)
    residual_block = lax.dynamic_slice_in_dim(residual, head_index * block_rows, block_rows)
    hidden_block = (residual_block.astype(jnp.float32) + share).astype(jnp.bfloat16)
    block_slots = (
        lax.dynamic_slice_in_dim(
            slot_rows.reshape(experts, n_expert, capacity), head_index * group, group, 1
        )
        - head_index * block_rows
    )
    gathered = jnp.take(
        hidden_block, block_slots.reshape(-1), axis=0, mode="fill", fill_value=0
    ).reshape(n_expert, local_experts * group * capacity, column_slab)
    received = lax.all_to_all(gathered, EXPERT, split_axis=0, concat_axis=2, tiled=True)
    arrived_rows = gather_all_axes(received, HEAD, 1)
    inputs = arrived_rows.astype(jnp.float32)
    inverse = lax.rsqrt(jnp.mean(inputs * inputs, axis=2, keepdims=True) + 1e-06)
    normed = (inputs * inverse * norm_gain.astype(jnp.float32)).astype(jnp.bfloat16)
    gate_act = jnp.einsum("esd,edf->esf", normed, w_gate, preferred_element_type=jnp.float32)
    up_act = jnp.einsum("esd,edf->esf", normed, w_up, preferred_element_type=jnp.float32)
    hidden_act = (jax.nn.silu(gate_act) * up_act).astype(jnp.bfloat16)
    partial_value = jnp.einsum(
        "esf,efd->esd", hidden_act, w_down, preferred_element_type=jnp.float32
    )
    shared = lax.psum_scatter(
        partial_value.astype(jnp.bfloat16), HEAD, scatter_dimension=1, tiled=True
    ).astype(jnp.float32)
    returned = lax.all_to_all(
        shared.astype(jnp.bfloat16), EXPERT, split_axis=2, concat_axis=0, tiled=True
    ).astype(shared.dtype)
    ids_block = lax.dynamic_slice_in_dim(expert_ids, head_index * block_rows, block_rows)
    gates_block = lax.dynamic_slice_in_dim(expert_gates, head_index * block_rows, block_rows)
    source_block = (
        lax.dynamic_slice_in_dim(
            source.reshape(rows_all, choose), head_index * block_rows, block_rows
        )
        - head_index * group
    )
    rank_block = lax.dynamic_slice_in_dim(
        ranking.reshape(rows_all, choose), head_index * block_rows, block_rows
    )
    local_slot = ids_block * (group * capacity) + source_block * capacity + rank_block
    picked = jnp.take(
        returned.reshape(experts * group * capacity, column_slab), local_slot.reshape(-1), axis=0
    ).reshape(block_rows, choose, column_slab)
    routed_block = jnp.sum(picked * gates_block[:, :, None], axis=1)
    return (hidden_block.astype(jnp.float32) + routed_block).astype(jnp.bfloat16)


def solution(mesh):
    finer = Mesh(mesh.devices.reshape(4, 2, 8, 4), ("head_0", "head_1", "expert_0", "expert_1"))
    in_specs = (
        P(EXPERT, HEAD, None),
        P(EXPERT, None, None),
        P(EXPERT),
        P(EXPERT, None, None),
        P(),
        P(),
        P(HEAD, None, None),
        P(HEAD, EXPERT),
        P(None, EXPERT),
        P(),
        P(),
        P(),
        P(EXPERT, None, HEAD),
        P(EXPERT, None, HEAD),
        P(EXPERT, HEAD, None),
    )
    out_specs = P(HEAD, EXPERT)
    return jax.shard_map(
        per_device, mesh=finer, in_specs=in_specs, out_specs=out_specs, check_vma=False
    )
```

profile of v0, /device:TPU:7, one launch (start us, length us, event | category | flops | bytes accessed | tf_op | source)
XLA Modules:
  0.0 369.7 jit_solution(5268701657149112454)
XLA Ops:
  6.5 0.9 dynamic_slice.29
  7.4 0.2 convert_reduce_fusion
  7.6 4.4 %sort.17 = (s32[384]{0:T(512)}, s32[384]{0:T(512)S(1)}) sort(s32[384]{0:T(512)} %param.20, s32[384]{0:T(512)S(1)} %iota.44), dimensions={0}, to_apply=%region_2.3 | sort | flops 3456 | bytes 6144 | tf_op jit(solution)/shard_map/jit(argsort)/sort | solution.py:142
  12.1 0.8 compare_select_fusion.8
  12.8 0.6 scatter_custom_fusion
  13.6 4.7 %gather_fusion.1 = bf16[64,64,576]{2,1,0:T(8,128)(2,1)} fusion(bf16[12,64,576]{2,1,0:T(8,128)(2,1)} %param.18, s32[1024]{0:T(1024)S(1)} %pad_clamp_fusion.3), kind=kCustom, calls=%fused_computation.1 | custom fusion | bytes 9437440 | tf_op jit(solution)/shard_map/jit(_take)/gather | solution.py:135
  18.3 1.4 dynamic-slice_select_fusion
  19.7 29.8 %all_to_all.37 = bf16[32,2,8,576]{3,2,1,0:T(8,128)(2,1)} all-to-all(bf16[32,2,8,576]{3,2,1,0:T(8,128)(2,1)S(1)} %dynamic-slice_select_fusion), channel_id=1, replica_groups=mesh['head_0'=4,'head_1'=2,'expert_0'=8,'expert_1'=4] {'expert_0','exper..., dimensions={0} | all-to-all | bytes 1179648 | tf_op jit(solution)/shard_map/all_to_all | solution.py:140
  49.6 0.7 gather_fusion
  50.3 0.2 convert_reduce_fusion.1
  50.5 1.2 fusion.24
  51.7 0.2 fusion.57
  51.8 0.4 convolution_convert_fusion.3
  52.2 0.4 fusion.27
  52.6 32.9 %all-gather.8.cloned.1.call-done = bf16[32,2,64,576]{3,2,1,0:T(8,128)(2,1)} async-done(((bf16[32,2,8,576]{3,2,1,0:T(8,128)(2,1)}), bf16[32,2,64,576]{3,2,1,0:T(8,128)(2,1)}) %all-gather.8.cloned.1.call-update) | async-done | bytes 4718608 | tf_op jit(solution)/shard_map/all_gather | solution.py:141
  85.5 3.2 gather_fusion.2
  88.7 0.2 broadcast_select_fusion
  88.9 0.9 copy-done.6
  89.9 0.4 fusion.20
  90.3 0.2 fusion.56
  90.5 1.6 convolution_convert_fusion.1
  92.1 0.5 fusion.26
  92.7 10.5 %all_gather.34 = bf16[64,2048]{1,0:T(8,128)(2,1)} all-gather(bf16[16,2048]{1,0:T(8,128)(2,1)S(1)} %pad_maximum_fusion.1), channel_id=1, replica_groups=mesh['head_0'=4,'head_1'=2,'expert_0'=8,'expert_1'=4] {'expert_1'}, dimensions={0}, use_global_device_ids=true | all-gather | bytes 327680 | tf_op jit(solution)/shard_map/all_gather | solution.py:16
  103.2 0.1 copy.95
  103.3 0.2 eq.47
  103.6 3.3 select_reduce_fusion
  107.0 0.1 copy.100
  107.1 0.2 mul.194
  107.5 15.5 %scatter_custom_fusion.1 = s32[6144]{0:T(1024)S(1)} fusion(s32[4096]{0:T(1024)S(1)} %bitcast.95, s32[4096]{0:T(1024)S(1)} %add_bitcast_fusion, s32[]{:T(128)} %constant.81.clone.1), kind=kCustom, calls=%fused_computation.75 | custom fusion | bytes 24580 | tf_op jit(solution)/shard_map/scatter | solution.py:167
  123.1 0.5 reshape.433
  123.6 0.1 reshape.435
  123.8 0.9 constant_dynamic-slice_fusion.2
  124.9 19.6 %all-gather.10.cloned.1.call-done = bf16[512,2048]{1,0:T(8,128)(2,1)} async-done(((bf16[64,2048]{1,0:T(8,128)(2,1)}), bf16[512,2048]{1,0:T(8,128)(2,1)}) %all-gather.10.cloned.1.call-update) | async-done | bytes 2097168 | tf_op jit(solution)/shard_map/all_gather | solution.py:16
  144.5 3.3 fusion.58
  147.9 8.8 %all-to-all-start.1 = ((f32[8,64,224]{2,1,0:T(8,128)}), f32[8,64,224]{2,1,0:T(8,128)S(1)}, u32[]{:S(2)}, u32[]{:S(2)}) async-start(f32[8,64,224]{2,1,0:T(8,128)} %bitcast.6), calls=%async_computation.1 | async-start | bytes 1048576 | tf_op jit(solution)/shard_map/all_to_all | solution.py:28
  156.8 7.6 %all-to-all-done.1 = f32[8,64,224]{2,1,0:T(8,128)S(1)} async-done(((f32[8,64,224]{2,1,0:T(8,128)}), f32[8,64,224]{2,1,0:T(8,128)S(1)}, u32[]{:S(2)}, u32[]{:S(2)}) %all-to-all-start.1) | async-done | bytes 458784 | tf_op jit(solution)/shard_map/all_to_all | solution.py:28
  164.5 2.7 gather_fusion.3
  167.2 0.2 broadcast_select_fusion.1
  167.4 20.6 %all_to_all.38 = bf16[32,24,224]{2,1,0:T(8,128)(2,1)S(1)} all-to-all(bf16[32,24,224]{2,1,0:T(8,128)(2,1)S(1)} %broadcast_select_fusion.1), channel_id=1, replica_groups=mesh['head_0'=4,'head_1'=2,'expert_0'=8,'expert_1'=4] {'expert_0','exper..., dimensions={0} | all-to-all | bytes 688128 | tf_op jit(solution)/shard_map/all_to_all | solution.py:181
  188.0 0.6 all_to_all.31
  188.7 4.4 %all-gather.2 = bf16[2,16,7168]{2,1,0:T(8,128)(2,1)} all-gather(bf16[1,16,7168]{2,1,0:T(8,128)(2,1)S(1)} %split.9), channel_id=4, replica_groups=mesh['head_0'=4,'head_1'=2,'expert_0'=8,'expert_1'=4] {'head_1'}, dimensions={0}, use_global_device_ids=true | all-gather | bytes 688128 | tf_op jit(solution)/shard_map/all_gather | solution.py:42
  193.3 11.5 %all-gather = bf16[4,8,7168]{2,1,0:T(8,128)(2,1)S(1)} all-gather(bf16[1,8,7168]{2,1,0:T(8,128)(2,1)S(1)} %split.8), channel_id=2, replica_groups=mesh['head_0'=4,'head_1'=2,'expert_0'=8,'expert_1'=4] {'head_0'}, dimensions={0}, use_global_device_ids=true | all-gather | bytes 573440 | tf_op jit(solution)/shard_map/all_gather | solution.py:42
  204.8 4.8 %all-gather.1 = bf16[8,8,7168]{2,1,0:T(8,128)(2,1)S(1)} all-gather(bf16[4,8,7168]{2,1,0:T(8,128)(2,1)S(1)} %all-gather), channel_id=3, replica_groups=mesh['head_0'=4,'head_1'=2,'expert_0'=8,'expert_1'=4] {'head_1'}, dimensions={0}, use_global_device_ids=true | all-gather | bytes 1376256 | tf_op jit(solution)/shard_map/all_gather | solution.py:42
  209.6 9.5 %all-gather.12.cloned.1.call-done = bf16[8,16,7168]{2,1,0:T(8,128)(2,1)} async-done(((bf16[2,16,7168]{2,1,0:T(8,128)(2,1)}), bf16[8,16,7168]{2,1,0:T(8,128)(2,1)}) %all-gather.12.cloned.1.call-update) | async-done | bytes 1835024 | tf_op jit(solution)/shard_map/all_gather | solution.py:42
  219.1 2.3 fusion.3
  221.4 0.8 fusion.5
  222.2 1.6 copy-done.2
  223.7 0.9 fusion.11
  224.6 6.1 %fusion.2 = bf16[1,192,7168]{2,1,0:T(8,128)(2,1)} fusion(bf16[1,128,7168]{2,1,0:T(8,128)(2,1)} %param.29, bf16[192,7168]{1,0:T(8,128)(2,1)} %bitcast.79, bf16[1,7168,128]{2,1,0:T(8,128)(2,1)} %param.28, f32[192,128]{1,0:T(8,128)S(1)} %fusion.11), kind=kOutput, calls=%fused_computation.10 | convolution fusion | flops 706166784 | bytes 9273344 | tf_op jit(solution)/shard_map/esf,efd->esd/dot_general | solution.py:189
  230.8 0.2 sub.55
  231.2 36.2 %reduce-scatter.2.cloned.1.call-done = bf16[1,24,7168]{2,1,0:T(8,128)(2,1)} async-done(((bf16[1,192,7168]{2,1,0:T(8,128)(2,1)}), bf16[1,24,7168]{2,1,0:T(8,128)(2,1)}) %reduce-scatter.2.cloned.1.call-update) | async-done | bytes 344080 | tf_op jit(solution)/shard_map/reduce_scatter | solution.py:192
  267.4 7.7 %copy.105 = bf16[1,24,7168]{1,0,2:T(2,128)(2,1)} copy(bf16[1,24,7168]{2,1,0:T(8,128)(2,1)} %reduce-scatter.2.cloned.1.call-done) | data formatting | bytes 688128 | tf_op jit(solution)/shard_map/reduce_scatter | solution.py:192
  275.1 0.5 broadcast.338
  275.6 41.0 %reduce.4 = bf16[7168,24]{1,0:T(8,128)(2,1)} reduce(bf16[7168,1,24]{2,1,0:T(2,128)(2,1)} %bitcast.81, bf16[]{:T(256)} %broadcast.338), dimensions={1}, to_apply=%bitcast.61.reduce_sub_computation | reduce | bytes 688130
  316.6 4.1 %reshape.513 = bf16[32,2,2688]{2,1,0:T(2,128)(2,1)} reshape(bf16[7168,24]{1,0:T(8,128)(2,1)} %reduce.4) | data formatting | bytes 688128
  320.7 9.4 %all-to-all-start.3 = ((bf16[32,2,2688]{2,1,0:T(2,128)(2,1)}), bf16[32,2,2688]{2,1,0:T(2,128)(2,1)S(1)}, u32[]{:S(2)}, u32[]{:S(2)}) async-start(bf16[32,2,2688]{2,1,0:T(2,128)(2,1)} %reshape.513), calls=%async_computation.4 | async-start | bytes 688128 | tf_op jit(solution)/shard_map/all_to_all | solution.py:195
  330.5 0.8 constant_dynamic-slice_fusion
  331.4 12.7 %all-to-all-done.3 = bf16[32,2,2688]{2,1,0:T(2,128)(2,1)S(1)} async-done(((bf16[32,2,2688]{2,1,0:T(2,128)(2,1)}), bf16[32,2,2688]{2,1,0:T(2,128)(2,1)S(1)}, u32[]{:S(2)}, u32[]{:S(2)}) %all-to-all-start.3) | async-done | bytes 344096 | tf_op jit(solution)/shard_map/all_to_all | solution.py:195
  344.0 6.2 %reshape.514 = bf16[7168,1,24]{2,1,0:T(2,128)(2,1)} reshape(bf16[32,2,2688]{2,1,0:T(2,128)(2,1)S(1)} %all-to-all-done.3) | data formatting | bytes 688128
  350.2 7.8 %bitcast_convert_fusion = f32[1,24,7168]{1,0,2:T(1,128)} fusion(bf16[7168,1,24]{2,1,0:T(2,128)(2,1)} %reshape.514), kind=kLoop, calls=%fused_computation.120 | loop fusion | flops 172032 | bytes 1032192 | tf_op jit(solution)/shard_map/convert_element_type | solution.py:197
  358.0 2.6 copy.106
  360.6 1.6 gather_fusion.4
  362.2 0.3 fusion.34
  362.5 0.6 add_convert_fusion
  (79 shorter events, 2.1 us)
Async XLA Ops:
  6.5 45.7 %copy-start = (bf16[16,512,128]{2,1,0:T(8,128)(2,1)S(1)}, bf16[16,512,128]{2,1,0:T(8,128)(2,1)}, u32[]{:S(2)}) copy-start(bf16[16,512,128]{2,1,0:T(8,128)(2,1)} %param.21) | copy-start | bytes 6291460
  6.5 79.0 %all-gather.8.cloned.1.call-start = ((), (), s32[]{:S(2)}) async-start(), calls=%async_computation.5 | async-start | bytes 5898240 | tf_op jit(solution)/shard_map/all_gather | solution.py:141
  18.3 31.3 %copy-start.1 = (s32[384]{0:T(512)S(1)}, s32[384]{0:T(512)}, u32[]{:S(2)}) copy-start(s32[384]{0:T(512)} %param.19) | copy-start | bytes 4612
  18.3 32.2 %copy-start.5 = (bf16[4,256,576]{1,2,0:T(8,128)(2,1)S(1)}, bf16[4,256,576]{1,2,0:T(8,128)(2,1)}, u32[]{:S(2)}) copy-start(bf16[4,256,576]{1,2,0:T(8,128)(2,1)} %param.16) | copy-start | bytes 3538948
  18.3 32.2 %copy-start.10 = (s32[4]{0:T(128)S(1)}, s32[4]{0:T(128)}, u32[]{:S(2)}) copy-start(s32[4]{0:T(128)} %param.17) | copy-start | bytes 52
  49.5 95.0 %all-gather.10.cloned.1.call-start = ((), (), s32[]{:S(2)}) async-start(), calls=%async_computation.6 | async-start | bytes 2359296 | tf_op jit(solution)/shard_map/all_gather | solution.py:16
  52.6 37.2 %copy-start.7 = (bf16[16,16,576]{2,1,0:T(8,128)(2,1)S(1)}, bf16[16,16,576]{2,1,0:T(8,128)(2,1)}, u32[]{:S(2)}) copy-start(bf16[16,16,576]{2,1,0:T(8,128)(2,1)} %param.15) | copy-start | bytes 884740
  88.9 1.0 copy-start.6
  90.5 12.7 %copy-start.8 = (s32[512,8]{0,1:T(8,128)S(1)}, s32[512,8]{0,1:T(8,128)}, u32[]{:S(2)}) copy-start(s32[512,8]{0,1:T(8,128)} %param.24) | copy-start | bytes 49156
  147.9 16.6 %all-to-all-start.1 = ((f32[8,64,224]{2,1,0:T(8,128)}), f32[8,64,224]{2,1,0:T(8,128)S(1)}, u32[]{:S(2)}, u32[]{:S(2)}) async-start(f32[8,64,224]{2,1,0:T(8,128)} %bitcast.6), calls=%async_computation.1 | async-start | bytes 1048576 | tf_op jit(solution)/shard_map/all_to_all | solution.py:28
  156.7 62.4 %all-gather.12.cloned.1.call-start = ((), (), s32[]{:S(2)}) async-start(), calls=%async_computation.8 | async-start | bytes 2293760 | tf_op jit(solution)/shard_map/all_gather | solution.py:42
  167.4 25.8 %copy-start.9 = (bf16[7168]{0:T(1024)(128)(2,1)S(1)}, bf16[7168]{0:T(1024)(128)(2,1)}, u32[]{:S(2)}) copy-start(bf16[7168]{0:T(1024)(128)(2,1)} %param.26) | copy-start | bytes 43012
  193.2 74.2 %reduce-scatter.2.cloned.1.call-start = ((), (), s32[]{:S(2)}) async-start(), calls=%async_computation.7 | async-start | bytes 3096576 | tf_op jit(solution)/shard_map/reduce_scatter | solution.py:192
  219.1 2.3 copy-start.3
  221.4 2.3 copy-start.4
  222.2 1.6 copy-start.2
  320.7 23.3 %all-to-all-start.3 = ((bf16[32,2,2688]{2,1,0:T(2,128)(2,1)}), bf16[32,2,2688]{2,1,0:T(2,128)(2,1)S(1)}, u32[]{:S(2)}, u32[]{:S(2)}) async-start(bf16[32,2,2688]{2,1,0:T(2,128)(2,1)} %reshape.513), calls=%async_computation.4 | async-start | bytes 688128 | tf_op jit(solution)/shard_map/all_to_all | solution.py:195
Sparse Core Ops, SparseCore 0:
  49.7 35.8 all-gather.7
  103.3 41.1 all-gather.9
  193.3 25.7 all-gather.11
  230.9 36.4 reduce-scatter.1
where the time goes:
time: 371 us; the launch traced here: 370 us
  waiting for transfers between devices  119 us (32%)
  blocking collectives  81.6 us (22%)
  other arithmetic  64.2 us (17%)
  local copies, waits for them, and re-layouts  58.6 us (16%)
  starting transfers between devices  18.3 us (5%)
  matrix products  14.8 us (4%)
  between operations  13.6 us (4%)
    unnamed x1, other arithmetic  41 us
    reduce_scatter x1, waiting for transfers between devices, per_device(): lax.psum_scatter(partial_value.astype(jnp.bfloat16), HEAD, scatter_dimens...  36.2 us
    all_gather x1, waiting for transfers between devices, per_device(): incoming = lax.all_gather(moved, HEAD, axis=2, tiled=True)  32.9 us
    all_to_all x1, blocking collectives, per_device(): lax.all_to_all(position_block, EXPERT, split_axis=0, concat_axis=0, tiled...  29.8 us
    all_gather x3, blocking collectives, gather_in_order(): pieces = lax.all_gather(pieces, axes[k])  20.8 us
    all_to_all x1, blocking collectives, per_device(): lax.all_to_all(gathered, EXPERT, split_axis=0, concat_axis=2, tiled=True)  20.6 us
    all_gather x1, waiting for transfers between devices, whole_of(): nearer = lax.all_gather(x, axes[-1], axis=dim, tiled=True)  19.6 us
    scatter x1, local copies, waits for them, and re-layouts, per_device(): slot_rows = jnp.full((experts * slots_all,), rows_all, jnp.int32).at[slot...  15.5 us
  transfers between devices with their start and end apart: 6, of which 6 were waited for; matrix products, arithmetic and copies ran while one was open for 7% of the time, Pallas kernels for 0%

commit v1 on v0

--- a/solution.py
+++ b/solution.py
@@ -138,7 +138,9 @@
     span = cache_shape[0] // n_head
     position_block = lax.dynamic_slice_in_dim(outgoing, head_index * span, span, 2)
     moved = lax.all_to_all(position_block, EXPERT, split_axis=0, concat_axis=0, tiled=True)
-    incoming = lax.all_gather(moved, HEAD, axis=2, tiled=True)
+    incoming = jnp.concatenate(
+        lax.all_to_all(jnp.stack([moved] * lax.axis_size(HEAD)), HEAD, 0, 0), axis=2
+    )
     ordering = jnp.argsort(new_owner, stable=True)
     chosen = lax.dynamic_slice_in_dim(ordering, owner_index * new_count, new_count)
     anchor = chosen // new_count

time: 371 us -> 402 us (1.084)
  waiting for transfers between devices: 119 us -> 136 us
  local copies, waits for them, and re-layouts: 58.6 us -> 66.8 us
  starting transfers between devices: 18.3 us -> 25.8 us
    all_to_all x0 -> x1, waiting for transfers between devices: none -> 55.4 us  [per_device(): lax.all_to_all(jnp.stack([moved] * lax.axis_size(HEAD)), HEAD, 0, 0)]
    all_gather x1 -> x0, waiting for transfers between devices: 32.9 us -> none  [per_device(): incoming = lax.all_gather(moved, HEAD, axis=2, tiled=True)]
    all_to_all x0 -> x1, starting transfers between devices: none -> 7.26 us  [per_device(): lax.all_to_all(jnp.stack([moved] * lax.axis_size(HEAD)), HEAD, 0, 0)]
    all_to_all x0 -> x1, local copies, waits for them, and re-layouts: none -> 5.7 us  [per_device(): lax.all_to_all(jnp.stack([moved] * lax.axis_size(HEAD)), HEAD, 0, 0)]
    all_gather x1, waiting for transfers between devices: 19.6 us -> 14.6 us  [whole_of(): nearer = lax.all_gather(x, axes[-1], axis=dim, tiled=True)]
    unnamed x30 -> x36, local copies, waits for them, and re-layouts: 13.7 us -> 13.2 us
where the time goes in v1:
time: 402 us; the launch traced here: 400 us
  waiting for transfers between devices  136 us (34%)
  blocking collectives  81.5 us (20%)
  local copies, waits for them, and re-layouts  66.8 us (17%)
  other arithmetic  62.9 us (16%)
  starting transfers between devices  25.8 us (6%)
  matrix products  14 us (3%)
  between operations  13.6 us (3%)
    all_to_all x1, waiting for transfers between devices, per_device(): lax.all_to_all(jnp.stack([moved] * lax.axis_size(HEAD)), HEAD, 0, 0)  55.4 us
    unnamed x1, other arithmetic  39.8 us
    reduce_scatter x1, waiting for transfers between devices, per_device(): lax.psum_scatter(partial_value.astype(jnp.bfloat16), HEAD, scatter_dimens...  36.2 us
    all_to_all x1, blocking collectives, per_device(): lax.all_to_all(position_block, EXPERT, split_axis=0, concat_axis=0, tiled...  29.7 us
    all_gather x3, blocking collectives, gather_in_order(): pieces = lax.all_gather(pieces, axes[k])  20.9 us
    all_to_all x1, blocking collectives, per_device(): lax.all_to_all(gathered, EXPERT, split_axis=0, concat_axis=2, tiled=True)  20.3 us
    scatter x1, local copies, waits for them, and re-layouts, per_device(): slot_rows = jnp.full((experts * slots_all,), rows_all, jnp.int32).at[slot...  15.5 us
    all_gather x1, waiting for transfers between devices, whole_of(): nearer = lax.all_gather(x, axes[-1], axis=dim, tiled=True)  14.6 us
  transfers between devices with their start and end apart: 6, of which 6 were waited for; matrix products, arithmetic and copies ran while one was open for 7% of the time, Pallas kernels for 0%

profile of v1, /device:TPU:7, one launch (start us, length us, event | category | flops | bytes accessed | tf_op | source)
XLA Modules:
  0.0 400.4 jit_solution(17403454844763706278)
XLA Ops:
  6.5 0.9 dynamic_slice.29
  7.4 0.2 convert_reduce_fusion
  7.6 4.4 %sort.17 = (s32[384]{0:T(512)}, s32[384]{0:T(512)S(1)}) sort(s32[384]{0:T(512)} %param.20, s32[384]{0:T(512)S(1)} %iota.44), dimensions={0}, to_apply=%region_2.3 | sort | flops 3456 | bytes 6144 | tf_op jit(solution)/shard_map/jit(argsort)/sort | solution.py:144
  12.1 0.8 compare_select_fusion.8
  12.8 0.6 scatter_custom_fusion
  13.6 4.7 %gather_fusion.1 = bf16[64,64,576]{2,1,0:T(8,128)(2,1)} fusion(bf16[12,64,576]{2,1,0:T(8,128)(2,1)} %param.18, s32[1024]{0:T(1024)S(1)} %pad_clamp_fusion.3), kind=kCustom, calls=%fused_computation.1 | custom fusion | bytes 9437440 | tf_op jit(solution)/shard_map/jit(_take)/gather | solution.py:135
  18.3 1.3 dynamic-slice_select_fusion
  19.6 29.7 %all_to_all.42 = bf16[32,2,8,576]{3,2,1,0:T(8,128)(2,1)S(1)} all-to-all(bf16[32,2,8,576]{3,2,1,0:T(8,128)(2,1)S(1)} %dynamic-slice_select_fusion), channel_id=1, replica_groups=mesh['head_0'=4,'head_1'=2,'expert_0'=8,'expert_1'=4] {'expert_0','exper..., dimensions={0} | all-to-all | bytes 1179648 | tf_op jit(solution)/shard_map/all_to_all | solution.py:140
  49.3 2.8 stack.2
  52.1 7.3 %all-to-all-start.1 = ((bf16[8,32,2,8,576]{4,3,2,1,0:T(8,128)(2,1)}), bf16[8,32,2,8,576]{4,3,2,1,0:T(8,128)(2,1)}, u32[]{:S(2)}, u32[]{:S(2)}) async-start(bf16[8,32,2,8,576]{4,3,2,1,0:T(8,128)(2,1)} %stack.2), calls=%async_computation.1 | async-start | bytes 10485760 | tf_op jit(solution)/shard_map/all_to_all | solution.py:142
  59.3 0.7 gather_fusion
  60.0 0.2 convert_reduce_fusion.1
  60.2 1.2 fusion.24
  61.4 0.2 fusion.57
  61.6 0.4 convolution_convert_fusion.3
  62.0 0.4 fusion.27
  62.4 55.4 %all-to-all-done.1 = bf16[8,32,2,8,576]{4,3,2,1,0:T(8,128)(2,1)} async-done(((bf16[8,32,2,8,576]{4,3,2,1,0:T(8,128)(2,1)}), bf16[8,32,2,8,576]{4,3,2,1,0:T(8,128)(2,1)}, u32[]{:S(2)}, u32[]{:S(2)}) %all-to-all-start.1) | async-done | bytes 4718624 | tf_op jit(solution)/shard_map/all_to_all | solution.py:142
  117.7 5.7 %copy.95 = bf16[8,32,2,8,576]{4,3,0,2,1:T(8,128)(2,1)} copy(bf16[8,32,2,8,576]{4,3,2,1,0:T(8,128)(2,1)} %all-to-all-done.1) | data formatting | bytes 9437184 | tf_op jit(solution)/shard_map/all_to_all | solution.py:142
  123.4 3.3 gather_fusion.2
  126.7 0.2 broadcast_select_fusion
  126.9 0.9 copy-done.8
  127.8 0.4 fusion.20
  128.2 0.2 fusion.56
  128.5 1.6 convolution_convert_fusion.1
  130.1 0.5 fusion.26
  130.6 10.5 %all_gather.30 = bf16[64,2048]{1,0:T(8,128)(2,1)} all-gather(bf16[16,2048]{1,0:T(8,128)(2,1)S(1)} %pad_maximum_fusion.1), channel_id=1, replica_groups=mesh['head_0'=4,'head_1'=2,'expert_0'=8,'expert_1'=4] {'expert_1'}, dimensions={0}, use_global_device_ids=true | all-gather | bytes 327680 | tf_op jit(solution)/shard_map/all_gather | solution.py:16
  141.6 3.3 select_reduce_fusion
  145.2 0.2 mul.194
  145.6 15.5 %scatter_custom_fusion.1 = s32[6144]{0:T(1024)S(1)} fusion(s32[4096]{0:T(1024)S(1)} %bitcast.97, s32[4096]{0:T(1024)S(1)} %add_bitcast_fusion, s32[]{:T(128)} %constant.81.clone.1), kind=kCustom, calls=%fused_computation.75 | custom fusion | bytes 24580 | tf_op jit(solution)/shard_map/scatter | solution.py:169
  161.1 0.5 reshape.435
  161.9 0.9 constant_dynamic-slice_fusion.2
  162.9 14.6 %all-gather.7.cloned.1.call-done = bf16[512,2048]{1,0:T(8,128)(2,1)} async-done(((bf16[64,2048]{1,0:T(8,128)(2,1)}), bf16[512,2048]{1,0:T(8,128)(2,1)}) %all-gather.7.cloned.1.call-update) | async-done | bytes 2097168 | tf_op jit(solution)/shard_map/all_gather | solution.py:16
  177.5 3.1 fusion.58
  180.6 9.1 %all-to-all-start.2 = ((f32[8,64,224]{2,1,0:T(8,128)}), f32[8,64,224]{2,1,0:T(8,128)S(1)}, u32[]{:S(2)}, u32[]{:S(2)}) async-start(f32[8,64,224]{2,1,0:T(8,128)} %bitcast.7), calls=%async_computation.2 | async-start | bytes 1048576 | tf_op jit(solution)/shard_map/all_to_all | solution.py:28
  189.8 7.6 %all-to-all-done.2 = f32[8,64,224]{2,1,0:T(8,128)S(1)} async-done(((f32[8,64,224]{2,1,0:T(8,128)}), f32[8,64,224]{2,1,0:T(8,128)S(1)}, u32[]{:S(2)}, u32[]{:S(2)}) %all-to-all-start.2) | async-done | bytes 458784 | tf_op jit(solution)/shard_map/all_to_all | solution.py:28
  197.5 2.7 gather_fusion.3
  200.2 0.2 broadcast_select_fusion.1
  200.4 20.3 %all_to_all.43 = bf16[32,24,224]{2,1,0:T(8,128)(2,1)S(1)} all-to-all(bf16[32,24,224]{2,1,0:T(8,128)(2,1)S(1)} %broadcast_select_fusion.1), channel_id=1, replica_groups=mesh['head_0'=4,'head_1'=2,'expert_0'=8,'expert_1'=4] {'expert_0','exper..., dimensions={0} | all-to-all | bytes 688128 | tf_op jit(solution)/shard_map/all_to_all | solution.py:183
  220.8 0.6 all_to_all.35
  221.4 4.4 %all-gather.2 = bf16[2,16,7168]{2,1,0:T(8,128)(2,1)} all-gather(bf16[1,16,7168]{2,1,0:T(8,128)(2,1)S(1)} %split.9), channel_id=4, replica_groups=mesh['head_0'=4,'head_1'=2,'expert_0'=8,'expert_1'=4] {'head_1'}, dimensions={0}, use_global_device_ids=true | all-gather | bytes 688128 | tf_op jit(solution)/shard_map/all_gather | solution.py:42
  226.0 11.5 %all-gather = bf16[4,8,7168]{2,1,0:T(8,128)(2,1)S(1)} all-gather(bf16[1,8,7168]{2,1,0:T(8,128)(2,1)S(1)} %split.8), channel_id=2, replica_groups=mesh['head_0'=4,'head_1'=2,'expert_0'=8,'expert_1'=4] {'head_0'}, dimensions={0}, use_global_device_ids=true | all-gather | bytes 573440 | tf_op jit(solution)/shard_map/all_gather | solution.py:42
  237.5 5.0 %all-gather.1 = bf16[8,8,7168]{2,1,0:T(8,128)(2,1)S(1)} all-gather(bf16[4,8,7168]{2,1,0:T(8,128)(2,1)S(1)} %all-gather), channel_id=3, replica_groups=mesh['head_0'=4,'head_1'=2,'expert_0'=8,'expert_1'=4] {'head_1'}, dimensions={0}, use_global_device_ids=true | all-gather | bytes 1376256 | tf_op jit(solution)/shard_map/all_gather | solution.py:42
  242.5 9.3 %all-gather.9.cloned.1.call-done = bf16[8,16,7168]{2,1,0:T(8,128)(2,1)} async-done(((bf16[2,16,7168]{2,1,0:T(8,128)(2,1)}), bf16[8,16,7168]{2,1,0:T(8,128)(2,1)}) %all-gather.9.cloned.1.call-update) | async-done | bytes 1835024 | tf_op jit(solution)/shard_map/all_gather | solution.py:42
  251.8 2.3 fusion.3
  254.1 0.8 fusion.5
  254.9 1.6 copy-done.3
  256.5 0.9 fusion.11
  257.3 0.6 copy-done.6
  258.0 5.6 %fusion.2 = bf16[1,192,7168]{2,1,0:T(8,128)(2,1)} fusion(bf16[1,128,7168]{2,1,0:T(8,128)(2,1)S(1)} %copy-done.6, bf16[192,7168]{1,0:T(8,128)(2,1)} %bitcast.81, bf16[1,7168,128]{2,1,0:T(8,128)(2,1)} %param.28, f32[192,128]{1,0:T(8,128)S(1)} %fusion.11), kind=kOutput, calls=%fused_computation.10 | convolution fusion | flops 706166784 | bytes 9273344 | tf_op jit(solution)/shard_map/esf,efd->esd/dot_general | solution.py:191
  263.6 0.2 sub.55
  263.9 36.2 %reduce-scatter.2.cloned.1.call-done = bf16[1,24,7168]{2,1,0:T(8,128)(2,1)} async-done(((bf16[1,192,7168]{2,1,0:T(8,128)(2,1)}), bf16[1,24,7168]{2,1,0:T(8,128)(2,1)}) %reduce-scatter.2.cloned.1.call-update) | async-done | bytes 344080 | tf_op jit(solution)/shard_map/reduce_scatter | solution.py:194
  300.2 7.7 %copy.109 = bf16[1,24,7168]{1,0,2:T(2,128)(2,1)} copy(bf16[1,24,7168]{2,1,0:T(8,128)(2,1)} %reduce-scatter.2.cloned.1.call-done) | data formatting | bytes 688128 | tf_op jit(solution)/shard_map/reduce_scatter | solution.py:194
  307.8 0.5 broadcast.340
  308.4 39.8 %reduce.4 = bf16[7168,24]{1,0:T(8,128)(2,1)S(1)} reduce(bf16[7168,1,24]{2,1,0:T(2,128)(2,1)} %bitcast.83, bf16[]{:T(256)} %broadcast.340), dimensions={1}, to_apply=%bitcast.63.reduce_sub_computation | reduce | bytes 688130
  348.1 3.1 reshape.515
  351.2 9.4 %all-to-all-start.4 = ((bf16[32,2,2688]{2,1,0:T(2,128)(2,1)}), bf16[32,2,2688]{2,1,0:T(2,128)(2,1)S(1)}, u32[]{:S(2)}, u32[]{:S(2)}) async-start(bf16[32,2,2688]{2,1,0:T(2,128)(2,1)} %reshape.515), calls=%async_computation.5 | async-start | bytes 688128 | tf_op jit(solution)/shard_map/all_to_all | solution.py:197
  361.0 0.8 constant_dynamic-slice_fusion
  361.9 12.7 %all-to-all-done.4 = bf16[32,2,2688]{2,1,0:T(2,128)(2,1)S(1)} async-done(((bf16[32,2,2688]{2,1,0:T(2,128)(2,1)}), bf16[32,2,2688]{2,1,0:T(2,128)(2,1)S(1)}, u32[]{:S(2)}, u32[]{:S(2)}) %all-to-all-start.4) | async-done | bytes 344096 | tf_op jit(solution)/shard_map/all_to_all | solution.py:197
  374.6 6.2 %reshape.516 = bf16[7168,1,24]{2,1,0:T(2,128)(2,1)} reshape(bf16[32,2,2688]{2,1,0:T(2,128)(2,1)S(1)} %all-to-all-done.4) | data formatting | bytes 688128
  380.8 7.8 %bitcast_convert_fusion = f32[1,24,7168]{1,0,2:T(1,128)} fusion(bf16[7168,1,24]{2,1,0:T(2,128)(2,1)} %reshape.516), kind=kLoop, calls=%fused_computation.120 | loop fusion | flops 172032 | bytes 1032192 | tf_op jit(solution)/shard_map/convert_element_type | solution.py:199
  388.6 2.8 copy.110
  391.4 1.6 gather_fusion.4
  392.9 0.3 fusion.34
  393.2 0.6 add_convert_fusion
  (86 shorter events, 2.6 us)
Async XLA Ops:
  6.5 55.4 %copy-start = (bf16[16,512,128]{2,1,0:T(8,128)(2,1)S(1)}, bf16[16,512,128]{2,1,0:T(8,128)(2,1)}, u32[]{:S(2)}) copy-start(bf16[16,512,128]{2,1,0:T(8,128)(2,1)} %param.21) | copy-start | bytes 6291460
  52.1 7.3 %copy-start.2 = (s32[384]{0:T(512)S(1)}, s32[384]{0:T(512)}, u32[]{:S(2)}) copy-start(s32[384]{0:T(512)} %param.19) | copy-start | bytes 4612
  52.1 8.2 %copy-start.7 = (bf16[4,256,576]{1,2,0:T(8,128)(2,1)S(1)}, bf16[4,256,576]{1,2,0:T(8,128)(2,1)}, u32[]{:S(2)}) copy-start(bf16[4,256,576]{1,2,0:T(8,128)(2,1)} %param.16) | copy-start | bytes 3538948
  52.1 8.2 %copy-start.12 = (s32[4]{0:T(128)S(1)}, s32[4]{0:T(128)}, u32[]{:S(2)}) copy-start(s32[4]{0:T(128)} %param.17) | copy-start | bytes 52
  52.1 65.7 %all-to-all-start.1 = ((bf16[8,32,2,8,576]{4,3,2,1,0:T(8,128)(2,1)}), bf16[8,32,2,8,576]{4,3,2,1,0:T(8,128)(2,1)}, u32[]{:S(2)}, u32[]{:S(2)}) async-start(bf16[8,32,2,8,576]{4,3,2,1,0:T(8,128)(2,1)} %stack.2), calls=%async_computation.1 | async-start | bytes 10485760 | tf_op jit(solution)/shard_map/all_to_all | solution.py:142
  59.3 118.2 %all-gather.7.cloned.1.call-start = ((), (), s32[]{:S(2)}) async-start(), calls=%async_computation.6 | async-start | bytes 2359296 | tf_op jit(solution)/shard_map/all_gather | solution.py:16
  123.4 4.4 %copy-start.9 = (bf16[16,16,576]{2,1,0:T(8,128)(2,1)S(1)}, bf16[16,16,576]{2,1,0:T(8,128)(2,1)}, u32[]{:S(2)}) copy-start(bf16[16,16,576]{2,1,0:T(8,128)(2,1)} %param.15) | copy-start | bytes 884740
  126.9 1.0 copy-start.8
  128.2 13.0 %copy-start.10 = (s32[512,8]{0,1:T(8,128)S(1)}, s32[512,8]{0,1:T(8,128)}, u32[]{:S(2)}) copy-start(s32[512,8]{0,1:T(8,128)} %param.24) | copy-start | bytes 49156
  130.1 47.4 %copy-start.13 = (bf16[2048,224]{0,1:T(8,128)(2,1)S(1)}, bf16[2048,224]{0,1:T(8,128)(2,1)}, u32[]{:S(2)}) copy-start(bf16[2048,224]{0,1:T(8,128)(2,1)} %param.22) | copy-start | bytes 2752516
  180.6 16.8 %all-to-all-start.2 = ((f32[8,64,224]{2,1,0:T(8,128)}), f32[8,64,224]{2,1,0:T(8,128)S(1)}, u32[]{:S(2)}, u32[]{:S(2)}) async-start(f32[8,64,224]{2,1,0:T(8,128)} %bitcast.7), calls=%async_computation.2 | async-start | bytes 1048576 | tf_op jit(solution)/shard_map/all_to_all | solution.py:28
  189.7 62.1 %all-gather.9.cloned.1.call-start = ((), (), s32[]{:S(2)}) async-start(), calls=%async_computation.8 | async-start | bytes 2293760 | tf_op jit(solution)/shard_map/all_gather | solution.py:42
  200.2 25.7 %copy-start.11 = (bf16[7168]{0:T(1024)(128)(2,1)S(1)}, bf16[7168]{0:T(1024)(128)(2,1)}, u32[]{:S(2)}) copy-start(bf16[7168]{0:T(1024)(128)(2,1)} %param.26) | copy-start | bytes 43012
  225.9 74.3 %reduce-scatter.2.cloned.1.call-start = ((), (), s32[]{:S(2)}) async-start(), calls=%async_computation.7 | async-start | bytes 3096576 | tf_op jit(solution)/shard_map/reduce_scatter | solution.py:194
  251.8 2.3 copy-start.4
  254.1 2.3 copy-start.5
  254.9 1.6 copy-start.3
  256.5 1.5 copy-start.6
  351.2 23.4 %all-to-all-start.4 = ((bf16[32,2,2688]{2,1,0:T(2,128)(2,1)}), bf16[32,2,2688]{2,1,0:T(2,128)(2,1)S(1)}, u32[]{:S(2)}, u32[]{:S(2)}) async-start(bf16[32,2,2688]{2,1,0:T(2,128)(2,1)} %reshape.515), calls=%async_computation.5 | async-start | bytes 688128 | tf_op jit(solution)/shard_map/all_to_all | solution.py:197
  388.6 5.3 %copy-start.1 = (bf16[16,512,128]{2,1,0:T(8,128)(2,1)S(1)}, bf16[16,512,128]{2,1,0:T(8,128)(2,1)}, u32[]{:S(2)}) copy-start(bf16[16,512,128]{2,1,0:T(8,128)(2,1)} %param.21) | copy-start | bytes 6291460
Sparse Core Ops, SparseCore 0:
  141.3 36.1 all-gather.6
  226.0 25.7 all-gather.8
  263.7 36.4 reduce-scatter.1
